TPU v7x, 32 devices: a whole 2x2x4 slice. The times are simulated.
32 devices in a mesh: group: 2 (over x), frame: 16 (over z, y, core).
Axes of the slice: x: 2, y: 2, z: 4, core: 2. Of those that a mesh axis runs over, the one named last changes fastest.
Arguments:
- queries: bfloat16 [10240, 5120], P(('group', 'frame')), parts along dimension 0, may hold values from -33 to 33
- keys: bfloat16 [10240, 5120], P(('group', 'frame')), parts along dimension 0, may hold values from -33 to 33
- values: bfloat16 [10240, 5120], P(('group', 'frame')), parts along dimension 0, may hold values from -6 to 6
- labels: int32 [80], P('group'), parts along dimension 0, may hold values from 0 to 1, as said below
- band: int32 [80], P('group'), parts along dimension 0, may hold values from 2 to 4
Outputs:
- attended: bfloat16 [10240, 5120], P(('group', 'frame')), parts along dimension 0
There are 2 independent parts, one for each index of `group`. A program takes and returns all parts, laid end to end along the dimension named above; each array names one. Nothing has to cross between parts.
Inputs may be any that keep to these rules, and one draw needn't show every extreme that they name: `labels`: exactly 10 of the 40 heads carry 1, the others 0.
All inputs are finite; a program needn't handle non-finite values.
Results may differ from a plain program's by a relative error of at most 0.0049.
Values may be sent and summed in bfloat16 or wider, within the bound.
A program may use at most 128 MiB of HBM per device.

v0:
```python
import math
import jax
import jax.numpy as jnp
from jax import lax
from jax.sharding import PartitionSpec as P

TEMP_HEADS = 10


def from_partner(block, axis, bit):
    count = lax.axis_size(axis)
    route = []
    for low in range(count):
        high = low | 1 << bit
        if high != low and high < count:
            route += [(low, high), (high, low)]
    return lax.ppermute(block, axis, route)


def softmax_rounded(scores):
    peak = jnp.max(scores, axis=-1, keepdims=True)
    weights = jnp.exp(scores - peak)
    return (weights / jnp.sum(weights, axis=-1, keepdims=True)).astype(jnp.bfloat16)


def block_heads(count):
    for candidate in (6, 5, 4, 3, 2):
        if count % candidate == 0:
            return candidate
    return 1


def attend_spatial(query_part, key_all, value_all):
    head_total = query_part.shape[1]
    step_heads = block_heads(head_total)
    scale = 1.0 / math.sqrt(query_part.shape[2])

    def one_block(block_number, result):
        start = block_number * step_heads
        query_block = lax.dynamic_slice_in_dim(query_part, start, step_heads, 1)
        key_block = lax.dynamic_slice_in_dim(key_all, start, step_heads, 1)
        value_block = lax.dynamic_slice_in_dim(value_all, start, step_heads, 1)
        scores = (
            jnp.einsum("rhd,khd->hrk", query_block, key_block, preferred_element_type=jnp.float32)
            * scale
        )
        weights = softmax_rounded(scores)
        output_block = jnp.einsum(
            "hrk,khd->rhd", weights, value_block, preferred_element_type=jnp.float32
        ).astype(jnp.bfloat16)
        return lax.dynamic_update_slice_in_dim(result, output_block, start, 1)

    initial = jnp.zeros(query_part.shape, jnp.bfloat16)
    return lax.fori_loop(0, head_total // step_heads, one_block, initial)


def attend_columns(query_part, key_part, value_part, head_band):
    query_cols, key_cols, value_cols = (
        lax.all_to_all(query_part[None], "frame", split_axis=1, concat_axis=0, tiled=True),
        lax.all_to_all(key_part[None], "frame", split_axis=1, concat_axis=0, tiled=True),
        lax.all_to_all(value_part[None], "frame", split_axis=1, concat_axis=0, tiled=True),
    )
    sources, pixels, head_part, head_size = query_cols.shape
    frames = sources // 2
    scale = 1.0 / math.sqrt(head_size)
    grid_shape = (frames, 2, pixels, head_part, head_size)
    scores = (
        jnp.einsum(
            "fapnd,gapnd->apnfg",
            query_cols.reshape(grid_shape),
            key_cols.reshape(grid_shape),
            preferred_element_type=jnp.float32,
        )
        * scale
    )
    frame_ids = jnp.arange(frames, dtype=jnp.int32)
    distance = jnp.abs(frame_ids[:, None] - frame_ids[None, :])
    keep = distance[None, :, :] <= head_band[:, None, None]
    scores = jnp.where(keep, scores, jnp.float32(-1e30))
    weights = softmax_rounded(scores)
    output = jnp.einsum(
        "apnfg,gapnd->fapnd",
        weights,
        value_cols.reshape(grid_shape),
        preferred_element_type=jnp.float32,
    ).astype(jnp.bfloat16)
    output = output.reshape(sources, pixels, head_part, head_size)
    returned = lax.all_to_all(output, "frame", split_axis=0, concat_axis=1, tiled=True)
    return returned[0]


def shards(queries, keys, values, labels, band):
    row_count = queries.shape[0]
    head_count = labels.shape[0]
    head_size = queries.shape[1] // head_count
    query_heads = queries.reshape(row_count, head_count, head_size)
    key_heads = keys.reshape(row_count, head_count, head_size)
    value_heads = values.reshape(row_count, head_count, head_size)
    spatial_count = head_count - TEMP_HEADS
    ordering = jnp.argsort(labels, stable=True)
    spatial_index = ordering[:spatial_count]
    temporal_index = ordering[spatial_count:]
    inverse = jnp.argsort(ordering, stable=True)
    query_spatial = jnp.take(query_heads, spatial_index, axis=1)
    key_spatial = jnp.take(key_heads, spatial_index, axis=1)
    value_spatial = jnp.take(value_heads, spatial_index, axis=1)
    temporal_band = jnp.take(band, temporal_index)
    temporal = attend_columns(
        jnp.take(query_heads, temporal_index, axis=1),
        jnp.take(key_heads, temporal_index, axis=1),
        jnp.take(value_heads, temporal_index, axis=1),
        temporal_band,
    )
    parity = lax.axis_index("frame") % 2
    half = spatial_count // 2
    mine_start = parity * half
    other_start = (1 - parity) * half
    query_mine = lax.dynamic_slice_in_dim(query_spatial, mine_start, half, 1)
    key_mine = lax.dynamic_slice_in_dim(key_spatial, mine_start, half, 1)
    value_mine = lax.dynamic_slice_in_dim(value_spatial, mine_start, half, 1)
    query_other = lax.dynamic_slice_in_dim(query_spatial, other_start, half, 1)
    key_other = lax.dynamic_slice_in_dim(key_spatial, other_start, half, 1)
    value_other = lax.dynamic_slice_in_dim(value_spatial, other_start, half, 1)
    query_got, key_got, value_got = from_partner((query_other, key_other, value_other), "frame", 0)

    def whole_frame(own, got):
        return jnp.where(
            parity == 0, jnp.concatenate([own, got], axis=0), jnp.concatenate([got, own], axis=0)
        )

    frame_out = attend_spatial(
        whole_frame(query_mine, query_got),
        whole_frame(key_mine, key_got),
        whole_frame(value_mine, value_got),
    )
    own_rows = lax.dynamic_slice_in_dim(frame_out, parity * row_count, row_count, 0)
    other_rows = lax.dynamic_slice_in_dim(frame_out, (1 - parity) * row_count, row_count, 0)
    returned = from_partner(other_rows, "frame", 0)
    spatial = jnp.where(
        parity == 0,
        jnp.concatenate([own_rows, returned], axis=1),
        jnp.concatenate([returned, own_rows], axis=1),
    )
    combined = jnp.take(jnp.concatenate([spatial, temporal], axis=1), inverse, axis=1)
    return combined.reshape(row_count, head_count * head_size)


def solution(mesh):
    placed = (
        P(("group", "frame"), None),
        P(("group", "frame"), None),
        P(("group", "frame"), None),
        P("group"),
        P("group"),
    )
    return jax.shard_map(
        shards, mesh=mesh, in_specs=placed, out_specs=P(("group", "frame"), None), check_vma=False
    )
```

profile of v0, /device:TPU:9, one launch (start us, length us, event | category | flops | bytes accessed | tf_op | source)
XLA Modules:
  0.0 212.5 jit_solution(6797831736654225508)
XLA Ops:
  0.0 1.9 copy-done
  1.9 2.6 %copy_bitcast_fusion.1 = bf16[320,40,128]{2,0,1:T(8,128)(2,1)} fusion(bf16[320,5120]{1,0:T(8,128)(2,1)S(1)} %copy-done), kind=kLoop, calls=%fused_computation.30 | loop fusion | bytes 6553600 | tf_op jit(solution)/shard_map/reshape | solution.py:96
  4.6 2.0 sort.31
  6.7 4.7 %copy_bitcast_fusion = bf16[320,40,128]{2,0,1:T(8,128)(2,1)} fusion(bf16[320,5120]{1,0:T(8,128)(2,1)} %param.12), kind=kLoop, calls=%fused_computation.29 | loop fusion | bytes 6553600 | tf_op jit(solution)/shard_map/reshape | solution.py:97
  11.3 1.6 gather_fusion.6
  13.0 3.5 %gather_fusion.7 = bf16[10,320,128]{2,1,0:T(8,128)(2,1)} fusion(bf16[320,40,128]{2,0,1:T(8,128)(2,1)} %copy_bitcast_fusion, s32[1024]{0:T(1024)S(1)} %pad_clamp_fusion.1), kind=kCustom, calls=%fused_computation.5.clone | custom fusion | bytes 1638440 | tf_op jit(solution)/shard_map/jit(_take)/gather | solution.py:110
  16.5 4.5 %copy_bitcast_fusion.2 = bf16[320,40,128]{2,0,1:T(8,128)(2,1)} fusion(bf16[320,5120]{1,0:T(8,128)(2,1)} %param.13), kind=kLoop, calls=%fused_computation.31 | loop fusion | bytes 6553600 | tf_op jit(solution)/shard_map/reshape | solution.py:98
  21.0 3.5 %gather_fusion.5 = bf16[10,320,128]{2,1,0:T(8,128)(2,1)} fusion(bf16[320,40,128]{2,0,1:T(8,128)(2,1)} %copy_bitcast_fusion.2, s32[1024]{0:T(1024)S(1)} %pad_clamp_fusion.1), kind=kCustom, calls=%fused_computation.1.clone | custom fusion | bytes 1638440 | tf_op jit(solution)/shard_map/jit(_take)/gather | solution.py:111
  24.6 3.1 %select_bitcast_fusion.4 = (bf16[1,320,10,128]{3,1,2,0:T(8,128)(2,1)}, bf16[1,320,10,128]{3,1,2,0:T(8,128)(2,1)S(1)}, bf16[1,320,10,128]{3,1,2,0:T(8,128)(2,1)}) fusion(bf16[10,320,128]{2,1,0:T(8,128)(2,1)} %gather_fusion.6, pred[10]{0:T(512)(128)(4,1)S(1)} %get-tuple-element.148, bf16[10,320,128]{2,1,0:T(8,128)(2,1)} %gather_fusion.7, ...), kind=kLoop, calls=%fused_computation.50 | loop fusion | flops 1228800 | bytes 4915210 | tf_op jit(solution)/shard_map/broadcast_in_dim | solution.py:59
  27.7 1.7 copy.97
  29.4 6.6 %all-to-all-start.2 = ((bf16[1,320,10,128]{3,2,0,1:T(8,128)(2,1)}), bf16[1,320,10,128]{3,2,0,1:T(8,128)(2,1)}, u32[]{:S(2)}, u32[]{:S(2)}) async-start(bf16[1,320,10,128]{3,2,0,1:T(8,128)(2,1)} %copy.97), calls=%async_computation.2 | async-start | bytes 2621440 | tf_op jit(solution)/shard_map/all_to_all | solution.py:60
  36.1 4.3 %gather_fusion.4 = bf16[30,320,128]{2,1,0:T(8,128)(2,1)} fusion(bf16[320,40,128]{2,0,1:T(8,128)(2,1)} %copy_bitcast_fusion, s32[1024]{0:T(1024)S(1)} %pad_clamp_fusion.2), kind=kCustom, calls=%fused_computation.3.clone | custom fusion | bytes 4915320 | tf_op jit(solution)/shard_map/jit(_take)/gather | solution.py:105
  40.4 2.3 %gather_fusion.3 = bf16[30,320,128]{2,1,0:T(8,128)(2,1)} fusion(bf16[320,40,128]{2,0,1:T(8,128)(2,1)S(1)} %copy-done.4, s32[1024]{0:T(1024)S(1)} %pad_clamp_fusion.2), kind=kCustom, calls=%fused_computation.2.clone | custom fusion | bytes 4915320 | tf_op jit(solution)/shard_map/jit(_take)/gather | solution.py:104
  42.7 4.4 %gather_fusion.2 = bf16[30,320,128]{2,1,0:T(8,128)(2,1)} fusion(bf16[320,40,128]{2,0,1:T(8,128)(2,1)} %copy_bitcast_fusion.2, s32[1024]{0:T(1024)S(1)} %pad_clamp_fusion.2), kind=kCustom, calls=%fused_computation.clone | custom fusion | bytes 4915320 | tf_op jit(solution)/shard_map/jit(_take)/gather | solution.py:106
  47.1 4.6 %select_bitcast_fusion = (bf16[320,30,128]{2,0,1:T(8,128)(2,1)}, bf16[320,30,128]{2,0,1:T(8,128)(2,1)S(1)}, bf16[320,30,128]{2,0,1:T(8,128)(2,1)S(1)}) fusion(bf16[30,320,128]{2,1,0:T(8,128)(2,1)S(1)} %copy-done.5, pred[30]{0:T(512)(128)(4,1)S(1)} %get-tuple-element.146, bf16[30,320,128]{2,1,0:T(8,128)(2,1)} %gather_fusion.3, ...), kind=kLoop, calls=%fused_computation.37 | loop fusion | flops 3686400 | bytes 14745630 | tf_op jit(solution)/shard_map/jit(_take)/select_n | solution.py:105
  51.7 1.6 constant_dynamic-slice_fusion.7
  53.6 1.6 constant_dynamic-slice_fusion.5
  55.4 1.7 copy.94
  57.1 9.3 %all-to-all-done.2 = bf16[1,320,10,128]{3,2,0,1:T(8,128)(2,1)} async-done(((bf16[1,320,10,128]{3,2,0,1:T(8,128)(2,1)}), bf16[1,320,10,128]{3,2,0,1:T(8,128)(2,1)}, u32[]{:S(2)}, u32[]{:S(2)}) %all-to-all-start.2) | async-done | bytes 819232 | tf_op jit(solution)/shard_map/all_to_all | solution.py:60
  66.3 5.2 %all-to-all-start.1 = ((bf16[1,320,10,128]{3,2,0,1:T(8,128)(2,1)}), bf16[1,320,10,128]{3,2,0,1:T(8,128)(2,1)}, u32[]{:S(2)}, u32[]{:S(2)}) async-start(bf16[1,320,10,128]{3,2,0,1:T(8,128)(2,1)} %copy.94), calls=%async_computation.1 | async-start | bytes 2621440 | tf_op jit(solution)/shard_map/all_to_all | solution.py:59
  71.6 1.6 constant_dynamic-slice_fusion.3
  73.6 2.8 %copy.91 = bf16[1,320,10,128]{3,2,0,1:T(8,128)(2,1)} copy(bf16[1,320,10,128]{3,1,2,0:T(8,128)(2,1)} %get-tuple-element.163) | data formatting | bytes 1638400 | tf_op jit(solution)/shard_map/broadcast_in_dim | solution.py:61
  76.4 0.7 gather_fusion
  77.2 4.0 %maximum_select_fusion = bf16[640,15,128]{2,0,1:T(8,128)(2,1)} fusion(bf16[320,15,128]{2,0,1:T(8,128)(2,1)} %collective-permute-done, bf16[320,15,128]{2,0,1:T(8,128)(2,1)S(1)} %copy-done.8, pred[]{:T(512)S(6)} %eq.4), kind=kLoop, calls=%fused_computation.33 | loop fusion | flops 11059200 | bytes 4915201 | tf_op jit(solution)/shard_map/jit(_where)/select_n | solution.py:127
  81.2 4.0 %maximum_select_fusion.1 = bf16[640,15,128]{2,0,1:T(8,128)(2,1)} fusion(bf16[320,15,128]{2,0,1:T(8,128)(2,1)} %collective-permute-done.1, bf16[320,15,128]{2,0,1:T(8,128)(2,1)S(1)} %copy-done.9, pred[]{:T(512)S(6)} %eq.4), kind=kLoop, calls=%fused_computation.34 | loop fusion | flops 11059200 | bytes 4915201 | tf_op jit(solution)/shard_map/jit(_where)/select_n | solution.py:127
  85.2 3.8 %maximum_select_fusion.2 = bf16[640,15,128]{2,0,1:T(8,128)(2,1)} fusion(bf16[320,15,128]{2,0,1:T(8,128)(2,1)} %collective-permute-done.2, bf16[320,15,128]{2,0,1:T(8,128)(2,1)S(1)} %copy-done.10, pred[]{:T(512)S(6)} %eq.4), kind=kLoop, calls=%fused_computation.35 | loop fusion | flops 11059200 | bytes 4915201 | tf_op jit(solution)/shard_map/jit(_where)/select_n | solution.py:127
  89.0 12.9 %all-to-all-done.1 = bf16[1,320,10,128]{3,2,0,1:T(8,128)(2,1)} async-done(((bf16[1,320,10,128]{3,2,0,1:T(8,128)(2,1)}), bf16[1,320,10,128]{3,2,0,1:T(8,128)(2,1)}, u32[]{:S(2)}, u32[]{:S(2)}) %all-to-all-start.1) | async-done | bytes 819232 | tf_op jit(solution)/shard_map/all_to_all | solution.py:59
  101.9 5.3 %all-to-all-start = ((bf16[1,320,10,128]{3,2,0,1:T(8,128)(2,1)}), bf16[1,320,10,128]{3,2,0,1:T(8,128)(2,1)S(1)}, u32[]{:S(2)}, u32[]{:S(2)}) async-start(bf16[1,320,10,128]{3,2,0,1:T(8,128)(2,1)} %copy.91), calls=%async_computation | async-start | bytes 2621440 | tf_op jit(solution)/shard_map/all_to_all | solution.py:61
  107.1 1.9 broadcast_in_dim.73.clone
  109.0 50.4 %while.13 = (s32[]{:T(128)}, bf16[640,15,128]{2,0,1:T(8,128)(2,1)}, bf16[640,15,128]{2,0,1:T(8,128)(2,1)}, bf16[640,15,128]{2,0,1:T(8,128)(2,1)}, bf16[640,15,12...) while((s32[]{:T(128)}, bf16[640,15,128]{2,0,1:T(8,128)(2,1)}, ...), condition=%wide.region_5.7_spmd, body=%wide.region_2.6_spmd.sunk | while | flops 1067422080 | bytes 72116400 | solution.py:54
  109.0 2.6 %fusion.48 = f32[5,640,640]{1,2,0:T(8,128)S(1)} fusion(bf16[640,15,128]{2,0,1:T(8,128)(2,1)} %get-tuple-element.219, s32[]{:T(128)S(6)} %select_n.164, bf16[640,15,128]{2,0,1:T(8,128)(2,1)} %get-tuple-element.218), kind=kOutput, calls=%fused_computation.17.clone.1 | convolution fusion | flops 524288000 | bytes 9831424 | tf_op jit(solution)/shard_map/while/body/eval_jaxpr/rhd,khd->hrk/dot_general | solution.py:44
  111.7 2.1 fusion.49
  113.8 1.0 copy-done.3
  114.8 8.7 %fusion.50 = bf16[640,5,128]{0,2,1:T(8,128)(2,1)S(1)} fusion(f32[5,640]{1,0:T(8,128)S(1)} %fusion.49, bf16[640,15,128]{2,0,1:T(8,128)(2,1)} %get-tuple-element.217, s32[]{:T(128)S(6)} %select_n.164, f32[5,640,640]{1,2,0:T(8,128)} %copy-done.3), kind=kOutput, calls=%fused_computation.16.clone.1 | convolution fusion | flops 534941440 | bytes 18035204 | tf_op jit(solution)/shard_map/while/body/eval_jaxpr/hrk,khd->rhd/dot_general | solution.py:48
  123.5 1.4 copy.137
  124.9 0.9 constant_dynamic-update-slice_fusion.2
  125.8 2.6 %fusion.48 = f32[5,640,640]{1,2,0:T(8,128)S(1)} fusion(bf16[640,15,128]{2,0,1:T(8,128)(2,1)} %get-tuple-element.219, s32[]{:T(128)S(6)} %select_n.164, bf16[640,15,128]{2,0,1:T(8,128)(2,1)} %get-tuple-element.218), kind=kOutput, calls=%fused_computation.17.clone.1 | convolution fusion | flops 524288000 | bytes 9831424 | tf_op jit(solution)/shard_map/while/body/eval_jaxpr/rhd,khd->hrk/dot_general | solution.py:44
  128.5 2.1 fusion.49
  130.6 1.0 copy-done.3
  131.6 8.7 %fusion.50 = bf16[640,5,128]{0,2,1:T(8,128)(2,1)S(1)} fusion(f32[5,640]{1,0:T(8,128)S(1)} %fusion.49, bf16[640,15,128]{2,0,1:T(8,128)(2,1)} %get-tuple-element.217, s32[]{:T(128)S(6)} %select_n.164, f32[5,640,640]{1,2,0:T(8,128)} %copy-done.3), kind=kOutput, calls=%fused_computation.16.clone.1 | convolution fusion | flops 534941440 | bytes 18035204 | tf_op jit(solution)/shard_map/while/body/eval_jaxpr/hrk,khd->rhd/dot_general | solution.py:48
  140.3 1.4 copy.137
  141.7 0.9 constant_dynamic-update-slice_fusion.2
  142.6 2.6 %fusion.48 = f32[5,640,640]{1,2,0:T(8,128)S(1)} fusion(bf16[640,15,128]{2,0,1:T(8,128)(2,1)} %get-tuple-element.219, s32[]{:T(128)S(6)} %select_n.164, bf16[640,15,128]{2,0,1:T(8,128)(2,1)} %get-tuple-element.218), kind=kOutput, calls=%fused_computation.17.clone.1 | convolution fusion | flops 524288000 | bytes 9831424 | tf_op jit(solution)/shard_map/while/body/eval_jaxpr/rhd,khd->hrk/dot_general | solution.py:44
  145.2 2.1 fusion.49
  147.4 1.0 copy-done.3
  148.4 8.7 %fusion.50 = bf16[640,5,128]{0,2,1:T(8,128)(2,1)S(1)} fusion(f32[5,640]{1,0:T(8,128)S(1)} %fusion.49, bf16[640,15,128]{2,0,1:T(8,128)(2,1)} %get-tuple-element.217, s32[]{:T(128)S(6)} %select_n.164, f32[5,640,640]{1,2,0:T(8,128)} %copy-done.3), kind=kOutput, calls=%fused_computation.16.clone.1 | convolution fusion | flops 534941440 | bytes 18035204 | tf_op jit(solution)/shard_map/while/body/eval_jaxpr/hrk,khd->rhd/dot_general | solution.py:48
  157.1 1.4 copy.137
  158.5 0.9 constant_dynamic-update-slice_fusion.2
  159.4 4.2 %exponential_reduce_fusion = (f32[2,20,10,8]{3,2,1,0:T(8,128)}, f32[2,20,10,8,8]{3,4,2,1,0:T(8,128)S(1)}) fusion(bf16[8,2,20,10,128]{4,3,2,1,0:T(8,128)(2,1)} %bitcast.13, bf16[8,2,20,10,128]{4,3,2,1,0:T(8,128)(2,1)} %bitcast.10, pred[10,8,8]{1,2,0:T(8,128)(4,1)S(1)} %broadcast_compare_fusion), kind=kOutput, calls=%fused_computation.43 | convolution fusion | flops 6656007 | bytes 1754240 | tf_op jit(solution)/shard_map/sub | solution.py:22
  163.6 1.8 fusion.24
  165.5 1.3 copy.103
  166.7 1.3 copy.104
  168.0 6.0 %all-to-all-start.3 = ((bf16[16,20,10,128]{3,1,2,0:T(8,128)(2,1)}), bf16[16,20,10,128]{3,1,2,0:T(8,128)(2,1)}, u32[]{:S(2)}, u32[]{:S(2)}) async-start(bf16[16,20,10,128]{3,1,2,0:T(8,128)(2,1)} %copy.104), calls=%async_computation.3 | async-start | bytes 1966080 | tf_op jit(solution)/shard_map/all_to_all | solution.py:88
  174.1 1.6 constant_dynamic-slice_fusion.1
  176.1 2.1 sort.32
  178.2 0.6 collective-permute-done.3
  178.8 1.0 copy-done.12
  179.9 2.7 %maximum_select_fusion.3 = bf16[320,30,128]{2,0,1:T(8,128)(2,1)S(1)} fusion(bf16[320,15,128]{2,0,1:T(8,128)(2,1)} %copy-done.12, bf16[320,15,128]{2,0,1:T(8,128)(2,1)} %get-tuple-element.150, pred[]{:T(512)S(6)} %eq.4), kind=kLoop, calls=%fused_computation.36 | loop fusion | flops 3686400 | bytes 4915201 | tf_op jit(solution)/shard_map/jit(_where)/select_n | solution.py:139
  182.6 15.1 %all-to-all-done.3 = bf16[16,20,10,128]{3,1,2,0:T(8,128)(2,1)} async-done(((bf16[16,20,10,128]{3,1,2,0:T(8,128)(2,1)}), bf16[16,20,10,128]{3,1,2,0:T(8,128)(2,1)}, u32[]{:S(2)}, u32[]{:S(2)}) %all-to-all-start.3) | async-done | bytes 819232 | tf_op jit(solution)/shard_map/all_to_all | solution.py:88
  197.7 2.4 %copy.105 = bf16[16,20,10,128]{3,1,0,2:T(8,128)(2,1)} copy(bf16[16,20,10,128]{3,1,2,0:T(8,128)(2,1)} %all-to-all-done.3) | data formatting | bytes 1638400 | tf_op jit(solution)/shard_map/all_to_all | solution.py:88
  200.0 1.3 squeeze.3
  201.3 2.0 pad_maximum_fusion
  203.3 4.9 %gather_fusion.1 = bf16[40,320,128]{2,1,0:T(8,128)(2,1)} fusion(bf16[320,40,128]{2,0,1:T(8,128)(2,1)} %pad_maximum_fusion, s32[1024]{0:T(1024)S(1)} %pad_clamp_fusion), kind=kCustom, calls=%fused_computation.7 | custom fusion | bytes 6553760 | tf_op jit(solution)/shard_map/jit(_take)/gather | solution.py:144
  208.2 4.3 %bitcast_select_fusion = bf16[320,5120]{1,0:T(8,128)(2,1)} fusion(pred[5120]{0:T(1024)(128)(4,1)S(1)} %broadcast_bitcast_fusion, bf16[40,320,128]{2,1,0:T(8,128)(2,1)} %gather_fusion.1), kind=kLoop, calls=%fused_computation.28 | loop fusion | flops 1638400 | bytes 6558720 | tf_op jit(solution)/shard_map/jit(_take)/select_n | solution.py:144
  (48 shorter events, 1.6 us)
Async XLA Ops:
  0.0 1.9 copy-start
  0.0 4.5 %copy-start.13 = (s32[40]{0:T(128)S(1)}, s32[40]{0:T(128)}, u32[]{:S(2)}) copy-start(s32[40]{0:T(128)} %param.14) | copy-start | bytes 484
  6.7 4.7 %copy-start.4 = (bf16[320,40,128]{2,0,1:T(8,128)(2,1)S(1)}, bf16[320,40,128]{2,0,1:T(8,128)(2,1)}, u32[]{:S(2)}) copy-start(bf16[320,40,128]{2,0,1:T(8,128)(2,1)} %copy_bitcast_fusion.1) | copy-start | bytes 9830404
  29.4 36.9 %all-to-all-start.2 = ((bf16[1,320,10,128]{3,2,0,1:T(8,128)(2,1)}), bf16[1,320,10,128]{3,2,0,1:T(8,128)(2,1)}, u32[]{:S(2)}, u32[]{:S(2)}) async-start(bf16[1,320,10,128]{3,2,0,1:T(8,128)(2,1)} %copy.97), calls=%async_computation.2 | async-start | bytes 2621440 | tf_op jit(solution)/shard_map/all_to_all | solution.py:60
  42.7 4.4 %copy-start.5 = (bf16[30,320,128]{2,1,0:T(8,128)(2,1)S(1)}, bf16[30,320,128]{2,1,0:T(8,128)(2,1)}, u32[]{:S(2)}) copy-start(bf16[30,320,128]{2,1,0:T(8,128)(2,1)} %gather_fusion.4) | copy-start | bytes 7372804
  53.3 23.9 %collective-permute-start = (bf16[320,15,128]{2,0,1:T(8,128)(2,1)}, bf16[320,15,128]{2,0,1:T(8,128)(2,1)}, u32[]{:S(2)}, u32[]{:S(2)}) collective-permute-start(bf16[320,15,128]{2,0,1:T(8,128)(2,1)} %get-tuple-element.157), channel_id=1, source_target_pairs={{0,1},{1,0},{2,3},{3,2},{4,5},{5,4},{6,7},{7,6},{8,9},{9,8},{10,11... | collective-permute-start | bytes 3686408 | tf_op jit(solution)/shard_map/ppermute | solution.py:17
  53.6 1.8 copy-start.11
  55.3 16.3 %copy-start.6 = (bf16[320,30,128]{2,0,1:T(8,128)(2,1)S(1)}, bf16[320,30,128]{2,0,1:T(8,128)(2,1)}, u32[]{:S(2)}) copy-start(bf16[320,30,128]{2,0,1:T(8,128)(2,1)} %get-tuple-element.158) | copy-start | bytes 7372804
  55.3 26.0 %collective-permute-start.1 = (bf16[320,15,128]{2,0,1:T(8,128)(2,1)}, bf16[320,15,128]{2,0,1:T(8,128)(2,1)}, u32[]{:S(2)}, u32[]{:S(2)}) collective-permute-start(bf16[320,15,128]{2,0,1:T(8,128)(2,1)} %get-tuple-element.155), channel_id=1, source_target_pairs={{0,1},{1,0},{2,3},{3,2},{4,5},{5,4},{6,7},{7,6},{8,9},{9,8},{10,11... | collective-permute-start | bytes 3686408 | tf_op jit(solution)/shard_map/ppermute | solution.py:17
  66.3 35.5 %all-to-all-start.1 = ((bf16[1,320,10,128]{3,2,0,1:T(8,128)(2,1)}), bf16[1,320,10,128]{3,2,0,1:T(8,128)(2,1)}, u32[]{:S(2)}, u32[]{:S(2)}) async-start(bf16[1,320,10,128]{3,2,0,1:T(8,128)(2,1)} %copy.94), calls=%async_computation.1 | async-start | bytes 2621440 | tf_op jit(solution)/shard_map/all_to_all | solution.py:59
  71.6 4.8 %copy-start.2 = (s32[40]{0:T(128)S(1)}, s32[40]{0:T(128)}, u32[]{:S(2)}) copy-start(s32[40]{0:T(128)} %param.15) | copy-start | bytes 484
  73.2 4.0 %copy-start.8 = (bf16[320,15,128]{2,0,1:T(8,128)(2,1)S(1)}, bf16[320,15,128]{2,0,1:T(8,128)(2,1)}, u32[]{:S(2)}) copy-start(bf16[320,15,128]{2,0,1:T(8,128)(2,1)} %get-tuple-element.156) | copy-start | bytes 3686404
  73.2 11.9 %collective-permute-start.2 = (bf16[320,15,128]{2,0,1:T(8,128)(2,1)}, bf16[320,15,128]{2,0,1:T(8,128)(2,1)}, u32[]{:S(2)}, u32[]{:S(2)}) collective-permute-start(bf16[320,15,128]{2,0,1:T(8,128)(2,1)} %get-tuple-element.153), channel_id=1, source_target_pairs={{0,1},{1,0},{2,3},{3,2},{4,5},{5,4},{6,7},{7,6},{8,9},{9,8},{10,11... | collective-permute-start | bytes 3686408 | tf_op jit(solution)/shard_map/ppermute | solution.py:17
  77.2 4.0 %copy-start.9 = (bf16[320,15,128]{2,0,1:T(8,128)(2,1)S(1)}, bf16[320,15,128]{2,0,1:T(8,128)(2,1)}, u32[]{:S(2)}) copy-start(bf16[320,15,128]{2,0,1:T(8,128)(2,1)} %get-tuple-element.154) | copy-start | bytes 3686404
  81.2 4.0 %copy-start.10 = (bf16[320,15,128]{2,0,1:T(8,128)(2,1)S(1)}, bf16[320,15,128]{2,0,1:T(8,128)(2,1)}, u32[]{:S(2)}) copy-start(bf16[320,15,128]{2,0,1:T(8,128)(2,1)} %get-tuple-element.152) | copy-start | bytes 3686404
  101.9 61.8 %all-to-all-start = ((bf16[1,320,10,128]{3,2,0,1:T(8,128)(2,1)}), bf16[1,320,10,128]{3,2,0,1:T(8,128)(2,1)S(1)}, u32[]{:S(2)}, u32[]{:S(2)}) async-start(bf16[1,320,10,128]{3,2,0,1:T(8,128)(2,1)} %copy.91), calls=%async_computation | async-start | bytes 2621440 | tf_op jit(solution)/shard_map/all_to_all | solution.py:61
  111.7 3.2 %copy-start.3 = (f32[5,640,640]{1,2,0:T(8,128)}, f32[5,640,640]{1,2,0:T(8,128)S(1)}, u32[]{:S(2)}) copy-start(f32[5,640,640]{1,2,0:T(8,128)S(1)} %fusion.48) | copy-start | bytes 24576004 | tf_op jit(solution)/shard_map/while
  128.4 3.2 %copy-start.3 = (f32[5,640,640]{1,2,0:T(8,128)}, f32[5,640,640]{1,2,0:T(8,128)S(1)}, u32[]{:S(2)}) copy-start(f32[5,640,640]{1,2,0:T(8,128)S(1)} %fusion.48) | copy-start | bytes 24576004 | tf_op jit(solution)/shard_map/while
  145.2 3.2 %copy-start.3 = (f32[5,640,640]{1,2,0:T(8,128)}, f32[5,640,640]{1,2,0:T(8,128)S(1)}, u32[]{:S(2)}) copy-start(f32[5,640,640]{1,2,0:T(8,128)S(1)} %fusion.48) | copy-start | bytes 24576004 | tf_op jit(solution)/shard_map/while
  165.5 8.6 %copy-start.7 = (bf16[640,15,128]{2,0,1:T(8,128)(2,1)S(1)}, bf16[640,15,128]{2,0,1:T(8,128)(2,1)}, u32[]{:S(2)}) copy-start(bf16[640,15,128]{2,0,1:T(8,128)(2,1)} %get-tuple-element.105) | copy-start | bytes 7372804
  168.0 29.6 %all-to-all-start.3 = ((bf16[16,20,10,128]{3,1,2,0:T(8,128)(2,1)}), bf16[16,20,10,128]{3,1,2,0:T(8,128)(2,1)}, u32[]{:S(2)}, u32[]{:S(2)}) async-start(bf16[16,20,10,128]{3,1,2,0:T(8,128)(2,1)} %copy.104), calls=%async_computation.3 | async-start | bytes 1966080 | tf_op jit(solution)/shard_map/all_to_all | solution.py:88
  175.7 3.1 %collective-permute-start.3 = (bf16[320,15,128]{2,0,1:T(8,128)(2,1)}, bf16[320,15,128]{2,0,1:T(8,128)(2,1)S(1)}, u32[]{:S(2)}, u32[]{:S(2)}) collective-permute-start(bf16[320,15,128]{2,0,1:T(8,128)(2,1)} %get-tuple-element.151), channel_id=1, source_target_pairs={{0,1},{1,0},{2,3},{3,2},{4,5},{5,4},{6,7},{7,6},{8,9},{9,8},{10,11... | collective-permute-start | bytes 3686408 | tf_op jit(solution)/shard_map/ppermute | solution.py:17
  178.8 1.0 copy-start.12
  203.3 9.2 %copy-start.1 = (bf16[320,5120]{1,0:T(8,128)(2,1)S(1)}, bf16[320,5120]{1,0:T(8,128)(2,1)}, u32[]{:S(2)}) copy-start(bf16[320,5120]{1,0:T(8,128)(2,1)} %param.11) | copy-start | bytes 9830404
where the time goes:
time: 213 us
  local copies, waits for them, and re-layouts  71.1 us (33%)
  matrix products  39.9 us (19%)
  other arithmetic  39.1 us (18%)
  waiting for transfers between devices  37.8 us (18%)
  starting transfers between devices  24.4 us (11%)
    dot_general x3, matrix products, one_block(): jnp.einsum('hrk,khd->rhd', weights, value_block, preferred_element_type=j...  26 us
    all_to_all x1, waiting for transfers between devices, attend_columns(): lax.all_to_all(output, 'frame', split_axis=0, concat_axis=1, tiled=True)  15.1 us
    all_to_all x1, waiting for transfers between devices, attend_columns(): lax.all_to_all(query_part[None], 'frame', split_axis=1, concat_axis=0, ti...  12.9 us
    select_n x3, other arithmetic, whole_frame(): jnp.where(parity == 0, jnp.concatenate([own, got], axis=0), jnp.concatena...  11.7 us
    all_to_all x1, waiting for transfers between devices, attend_columns(): lax.all_to_all(key_part[None], 'frame', split_axis=1, concat_axis=0, tile...  9.25 us
    dot_general x3, matrix products, one_block(): jnp.einsum('rhd,khd->hrk', query_block, key_block, preferred_element_type...  7.85 us
    dynamic_update_slice x6, local copies, waits for them, and re-layouts, one_block(): return lax.dynamic_update_slice_in_dim(result, output_block, start, 1)  7.02 us
    all_to_all x1, starting transfers between devices, attend_columns(): lax.all_to_all(key_part[None], 'frame', split_axis=1, concat_axis=0, tile...  6.61 us
  transfers between devices with their start and end apart: 8, of which 4 were waited for; matrix products, arithmetic and copies ran while one was open for 46% of the time, Pallas kernels for 0%

commit v1 on v0

--- a/solution.py
+++ b/solution.py
@@ -3,8 +3,30 @@
 import jax.numpy as jnp
 from jax import lax
 from jax.sharding import PartitionSpec as P
+from jax.lax import axis_index, axis_size, ppermute
 
 TEMP_HEADS = 10
+
+
+def expand_sheets(view, dim_no, sample):
+    arr_next = view.shape
+    shaped = jnp.moveaxis(
+        view.reshape(
+            *arr_next[:dim_no], sample, arr_next[dim_no] // sample, *arr_next[dim_no + 1 :]
+        ),
+        dim_no,
+        0,
+    )
+    return shaped
+
+
+def _work_trees(x0, axis_k):
+    x0 = jnp.moveaxis(x0, 0, axis_k)
+    work_now = x0.shape
+    block_next = x0.reshape(
+        *work_now[:axis_k], work_now[axis_k] * work_now[axis_k + 1], *work_now[axis_k + 2 :]
+    )
+    return block_next
 
 
 def from_partner(block, axis, bit):
@@ -85,7 +107,14 @@
         preferred_element_type=jnp.float32,
     ).astype(jnp.bfloat16)
     output = output.reshape(sources, pixels, head_part, head_size)
-    returned = lax.all_to_all(output, "frame", split_axis=0, concat_axis=1, tiled=True)
+    y2, block_last = (axis_size("frame"), axis_index("frame"))
+    later = expand_sheets(output, 0, y2)
+    grid = [later[block_last]]
+    for i0 in range(1, y2):
+        t_next = later[block_last ^ i0]
+        grid.append(ppermute(t_next, "frame", [(nth, nth ^ i0) for nth in range(y2)]))
+    later = jnp.stack(grid, 0)[block_last ^ jnp.arange(y2)]
+    returned = _work_trees(later, 1)
     return returned[0]
 
 

time: 213 us -> 220 us (1.033)
  starting transfers between devices: 24.4 us -> 35 us
  waiting for transfers between devices: 37.8 us -> 32.6 us
  local copies, waits for them, and re-layouts: 71.1 us -> 67.7 us
    ppermute x0 -> x15, starting transfers between devices: none -> 16.9 us  [attend_columns(): ppermute(t_next, 'frame', [(nth, nth ^ i0) for nth in range(y2)])]
    ppermute x0 -> x15, waiting for transfers between devices: none -> 15.3 us  [attend_columns(): ppermute(t_next, 'frame', [(nth, nth ^ i0) for nth in range(y2)])]
    all_to_all x1 -> x0, waiting for transfers between devices: 15.1 us -> none  [attend_columns(): lax.all_to_all(output, 'frame', split_axis=0, concat_axis=1, tiled=True)]
    all_to_all x1, waiting for transfers between devices: 9.25 us -> 1.54 us  [attend_columns(): lax.all_to_all(key_part[None], 'frame', split_axis=1, concat_axis=0, tile...]
    all_to_all x1 -> x0, starting transfers between devices: 6.02 us -> none  [attend_columns(): lax.all_to_all(output, 'frame', split_axis=0, concat_axis=1, tiled=True)]
    all_to_all x1, waiting for transfers between devices: 12.9 us -> 15.8 us  [attend_columns(): lax.all_to_all(query_part[None], 'frame', split_axis=1, concat_axis=0, ti...]
    all_to_all x1 -> x0, local copies, waits for them, and re-layouts: 2.36 us -> none  [attend_columns(): lax.all_to_all(output, 'frame', split_axis=0, concat_axis=1, tiled=True)]
  transfers between devices with their start and end apart: 8 -> 22, of which waited for: 4 -> 10; matrix products, arithmetic and copies ran while one was open for 46% -> 48% of each run, Pallas kernels for 0% -> 0%
where the time goes in v1:
time: 220 us; the launch traced here: 218 us
  local copies, waits for them, and re-layouts  67.7 us (31%)
  other arithmetic  41 us (19%)
  matrix products  40.8 us (19%)
  starting transfers between devices  35 us (16%)
  waiting for transfers between devices  32.6 us (15%)
    dot_general x3, matrix products, one_block(): jnp.einsum('hrk,khd->rhd', weights, value_block, preferred_element_type=j...  26 us
    ppermute x15, starting transfers between devices, attend_columns(): ppermute(t_next, 'frame', [(nth, nth ^ i0) for nth in range(y2)])  16.9 us
    all_to_all x1, waiting for transfers between devices, attend_columns(): lax.all_to_all(query_part[None], 'frame', split_axis=1, concat_axis=0, ti...  15.8 us
    ppermute x15, waiting for transfers between devices, attend_columns(): ppermute(t_next, 'frame', [(nth, nth ^ i0) for nth in range(y2)])  15.3 us
    select_n x3, other arithmetic, whole_frame(): jnp.where(parity == 0, jnp.concatenate([own, got], axis=0), jnp.concatena...  11.8 us
    dot_general x3, matrix products, one_block(): jnp.einsum('rhd,khd->hrk', query_block, key_block, preferred_element_type...  7.84 us
    dynamic_update_slice x6, local copies, waits for them, and re-layouts, one_block(): return lax.dynamic_update_slice_in_dim(result, output_block, start, 1)  7.02 us
    all_to_all x1, starting transfers between devices, attend_columns(): lax.all_to_all(key_part[None], 'frame', split_axis=1, concat_axis=0, tile...  6.61 us
  transfers between devices with their start and end apart: 22, of which 10 were waited for; matrix products, arithmetic and copies ran while one was open for 48% of the time, Pallas kernels for 0%

profile of v1, /device:TPU:9, one launch (start us, length us, event | category | flops | bytes accessed | tf_op | source)
XLA Modules:
  0.0 217.8 jit_solution(14193096866032544922)
XLA Ops:
  0.0 2.8 %sort.31 = (s32[40]{0:T(128)}, s32[40]{0:T(128)S(1)}) sort(s32[40]{0:T(128)} %param.14, s32[40]{0:T(128)S(1)} %iota.25), dimensions={0}, to_apply=%region_0.0 | sort | flops 240 | bytes 640 | tf_op jit(solution)/shard_map/jit(argsort)/sort | solution.py:129
  3.0 2.6 %copy_bitcast_fusion.1 = bf16[320,40,128]{2,0,1:T(8,128)(2,1)} fusion(bf16[320,5120]{1,0:T(8,128)(2,1)S(1)} %copy-done), kind=kLoop, calls=%fused_computation.31 | loop fusion | bytes 6553600 | tf_op jit(solution)/shard_map/reshape | solution.py:125
  5.6 2.6 %copy_bitcast_fusion = bf16[320,40,128]{2,0,1:T(8,128)(2,1)} fusion(bf16[320,5120]{1,0:T(8,128)(2,1)S(1)} %copy-done.13), kind=kLoop, calls=%fused_computation.30 | loop fusion | bytes 6553600 | tf_op jit(solution)/shard_map/reshape | solution.py:126
  8.2 1.6 gather_fusion.7
  9.8 3.5 %gather_fusion.8 = bf16[10,320,128]{2,1,0:T(8,128)(2,1)} fusion(bf16[320,40,128]{2,0,1:T(8,128)(2,1)} %copy_bitcast_fusion, s32[1024]{0:T(1024)S(1)} %get-tuple-element.177), kind=kCustom, calls=%fused_computation.5.clone | custom fusion | bytes 1638440 | tf_op jit(solution)/shard_map/jit(_take)/gather | solution.py:139
  13.3 4.5 %copy_bitcast_fusion.2 = bf16[320,40,128]{2,0,1:T(8,128)(2,1)} fusion(bf16[320,5120]{1,0:T(8,128)(2,1)} %param.13), kind=kLoop, calls=%fused_computation.32 | loop fusion | bytes 6553600 | tf_op jit(solution)/shard_map/reshape | solution.py:127
  17.8 3.5 %gather_fusion.6 = bf16[10,320,128]{2,1,0:T(8,128)(2,1)} fusion(bf16[320,40,128]{2,0,1:T(8,128)(2,1)} %copy_bitcast_fusion.2, s32[1024]{0:T(1024)S(1)} %get-tuple-element.177), kind=kCustom, calls=%fused_computation.1.clone | custom fusion | bytes 1638440 | tf_op jit(solution)/shard_map/jit(_take)/gather | solution.py:140
  21.4 3.1 %select_bitcast_fusion.4 = (bf16[1,320,10,128]{3,1,2,0:T(8,128)(2,1)}, bf16[1,320,10,128]{3,1,2,0:T(8,128)(2,1)S(1)}, bf16[1,320,10,128]{3,1,2,0:T(8,128)(2,1)}) fusion(bf16[10,320,128]{2,1,0:T(8,128)(2,1)} %gather_fusion.7, pred[10]{0:T(512)(128)(4,1)S(1)} %get-tuple-element.143, bf16[10,320,128]{2,1,0:T(8,128)(2,1)} %gather_fusion.8, ...), kind=kLoop, calls=%fused_computation.51 | loop fusion | flops 1228800 | bytes 4915210 | tf_op jit(solution)/shard_map/broadcast_in_dim | solution.py:81
  24.4 1.7 copy.120
  26.2 6.6 %all-to-all-start.2 = ((bf16[1,320,10,128]{3,2,0,1:T(8,128)(2,1)}), bf16[1,320,10,128]{3,2,0,1:T(8,128)(2,1)}, u32[]{:S(2)}, u32[]{:S(2)}) async-start(bf16[1,320,10,128]{3,2,0,1:T(8,128)(2,1)} %copy.120), calls=%async_computation.2 | async-start | bytes 2621440 | tf_op jit(solution)/shard_map/all_to_all | solution.py:82
  32.8 4.3 %gather_fusion.5 = bf16[30,320,128]{2,1,0:T(8,128)(2,1)} fusion(bf16[320,40,128]{2,0,1:T(8,128)(2,1)} %copy_bitcast_fusion, s32[1024]{0:T(1024)S(1)} %get-tuple-element.178), kind=kCustom, calls=%fused_computation.3.clone | custom fusion | bytes 4915320 | tf_op jit(solution)/shard_map/jit(_take)/gather | solution.py:134
  37.0 2.3 %gather_fusion.4 = bf16[30,320,128]{2,1,0:T(8,128)(2,1)} fusion(bf16[320,40,128]{2,0,1:T(8,128)(2,1)S(1)} %copy-done.4, s32[1024]{0:T(1024)S(1)} %get-tuple-element.178), kind=kCustom, calls=%fused_computation.2.clone | custom fusion | bytes 4915320 | tf_op jit(solution)/shard_map/jit(_take)/gather | solution.py:133
  39.4 4.4 %gather_fusion.3 = bf16[30,320,128]{2,1,0:T(8,128)(2,1)} fusion(bf16[320,40,128]{2,0,1:T(8,128)(2,1)} %copy_bitcast_fusion.2, s32[1024]{0:T(1024)S(1)} %get-tuple-element.178), kind=kCustom, calls=%fused_computation.clone | custom fusion | bytes 4915320 | tf_op jit(solution)/shard_map/jit(_take)/gather | solution.py:135
  43.8 5.8 %select_bitcast_fusion = (bf16[320,30,128]{2,0,1:T(8,128)(2,1)}, bf16[320,30,128]{2,0,1:T(8,128)(2,1)}, bf16[320,30,128]{2,0,1:T(8,128)(2,1)}) fusion(bf16[30,320,128]{2,1,0:T(8,128)(2,1)S(1)} %copy-done.5, pred[30]{0:T(512)(128)(4,1)S(1)} %get-tuple-element.141, bf16[30,320,128]{2,1,0:T(8,128)(2,1)} %gather_fusion.4, bf16[30,320,128]{2,1,0:T(8,128)(2,1)} %gather_fusion.3), kind=kLoop, calls=%fused_computation.38 | loop fusion | flops 3686400 | bytes 14745630 | tf_op jit(solution)/shard_map/jit(_take)/select_n | solution.py:134
  49.6 3.4 %constant_dynamic-slice_fusion.23 = (bf16[320,15,128]{2,0,1:T(8,128)(2,1)}, bf16[320,15,128]{2,0,1:T(8,128)(2,1)}) fusion(bf16[320,30,128]{2,0,1:T(8,128)(2,1)} %get-tuple-element.171, s32[]{:T(128)S(6)} %select_n.157, s32[]{:T(128)S(6)} %select_n.158), kind=kLoop, calls=%fused_computation.109 | loop fusion | bytes 4915208 | tf_op jit(solution)/shard_map/dynamic_slice | solution.py:149
  53.4 1.6 constant_dynamic-slice_fusion.21
  56.0 1.6 constant_dynamic-slice_fusion.19
  57.8 2.0 sort.32
  59.8 1.6 copy.117
  61.5 1.5 all-to-all-done.2
  63.1 5.2 %all-to-all-start.1 = ((bf16[1,320,10,128]{3,2,0,1:T(8,128)(2,1)}), bf16[1,320,10,128]{3,2,0,1:T(8,128)(2,1)}, u32[]{:S(2)}, u32[]{:S(2)}) async-start(bf16[1,320,10,128]{3,2,0,1:T(8,128)(2,1)} %copy.117), calls=%async_computation.1 | async-start | bytes 2621440 | tf_op jit(solution)/shard_map/all_to_all | solution.py:81
  68.4 1.6 copy.114
  71.0 4.0 %maximum_select_fusion = bf16[640,15,128]{2,0,1:T(8,128)(2,1)} fusion(bf16[320,15,128]{2,0,1:T(8,128)(2,1)} %collective-permute-done, bf16[320,15,128]{2,0,1:T(8,128)(2,1)S(1)} %copy-done.8, pred[]{:T(512)S(6)} %eq.4), kind=kLoop, calls=%fused_computation.34 | loop fusion | flops 11059200 | bytes 4915201 | tf_op jit(solution)/shard_map/jit(_where)/select_n | solution.py:156
  75.0 4.0 %maximum_select_fusion.1 = bf16[640,15,128]{2,0,1:T(8,128)(2,1)} fusion(bf16[320,15,128]{2,0,1:T(8,128)(2,1)} %collective-permute-done.1, bf16[320,15,128]{2,0,1:T(8,128)(2,1)S(1)} %copy-done.9, pred[]{:T(512)S(6)} %eq.4), kind=kLoop, calls=%fused_computation.35 | loop fusion | flops 11059200 | bytes 4915201 | tf_op jit(solution)/shard_map/jit(_where)/select_n | solution.py:156
  79.0 3.8 %maximum_select_fusion.2 = bf16[640,15,128]{2,0,1:T(8,128)(2,1)} fusion(bf16[320,15,128]{2,0,1:T(8,128)(2,1)} %collective-permute-done.2, bf16[320,15,128]{2,0,1:T(8,128)(2,1)S(1)} %copy-done.10, pred[]{:T(512)S(6)} %eq.4), kind=kLoop, calls=%fused_computation.36 | loop fusion | flops 11059200 | bytes 4915201 | tf_op jit(solution)/shard_map/jit(_where)/select_n | solution.py:156
  82.8 15.8 %all-to-all-done.1 = bf16[1,320,10,128]{3,2,0,1:T(8,128)(2,1)} async-done(((bf16[1,320,10,128]{3,2,0,1:T(8,128)(2,1)}), bf16[1,320,10,128]{3,2,0,1:T(8,128)(2,1)}, u32[]{:S(2)}, u32[]{:S(2)}) %all-to-all-start.1) | async-done | bytes 819232 | tf_op jit(solution)/shard_map/all_to_all | solution.py:81
  98.6 5.3 %all-to-all-start = ((bf16[1,320,10,128]{3,2,0,1:T(8,128)(2,1)}), bf16[1,320,10,128]{3,2,0,1:T(8,128)(2,1)S(1)}, u32[]{:S(2)}, u32[]{:S(2)}) async-start(bf16[1,320,10,128]{3,2,0,1:T(8,128)(2,1)} %copy.114), calls=%async_computation | async-start | bytes 2621440 | tf_op jit(solution)/shard_map/all_to_all | solution.py:83
  103.8 1.9 broadcast_in_dim.74.clone
  105.8 50.4 %while.13 = (s32[]{:T(128)}, bf16[640,15,128]{2,0,1:T(8,128)(2,1)}, bf16[640,15,128]{2,0,1:T(8,128)(2,1)}, bf16[640,15,128]{2,0,1:T(8,128)(2,1)}, bf16[640,15,12...) while((s32[]{:T(128)}, bf16[640,15,128]{2,0,1:T(8,128)(2,1)}, ...), condition=%wide.region_5.7_spmd, body=%wide.region_2.6_spmd.sunk | while | flops 1067422080 | bytes 72116400 | solution.py:76
  105.8 2.6 %fusion.49 = f32[5,640,640]{1,2,0:T(8,128)S(1)} fusion(bf16[640,15,128]{2,0,1:T(8,128)(2,1)} %get-tuple-element.232, s32[]{:T(128)S(6)} %select_n.242, bf16[640,15,128]{2,0,1:T(8,128)(2,1)} %get-tuple-element.231), kind=kOutput, calls=%fused_computation.18.clone.1 | convolution fusion | flops 524288000 | bytes 9831424 | tf_op jit(solution)/shard_map/while/body/eval_jaxpr/rhd,khd->hrk/dot_general | solution.py:66
  108.4 2.1 fusion.50
  111.6 8.7 %fusion.51 = bf16[640,5,128]{0,2,1:T(8,128)(2,1)S(1)} fusion(f32[5,640]{1,0:T(8,128)S(1)} %fusion.50, bf16[640,15,128]{2,0,1:T(8,128)(2,1)} %get-tuple-element.230, s32[]{:T(128)S(6)} %select_n.242, f32[5,640,640]{1,2,0:T(8,128)} %copy-done.3), kind=kOutput, calls=%fused_computation.17.clone.1 | convolution fusion | flops 534941440 | bytes 18035204 | tf_op jit(solution)/shard_map/while/body/eval_jaxpr/hrk,khd->rhd/dot_general | solution.py:70
  120.2 1.4 copy.207
  122.6 2.6 %fusion.49 = f32[5,640,640]{1,2,0:T(8,128)S(1)} fusion(bf16[640,15,128]{2,0,1:T(8,128)(2,1)} %get-tuple-element.232, s32[]{:T(128)S(6)} %select_n.242, bf16[640,15,128]{2,0,1:T(8,128)(2,1)} %get-tuple-element.231), kind=kOutput, calls=%fused_computation.18.clone.1 | convolution fusion | flops 524288000 | bytes 9831424 | tf_op jit(solution)/shard_map/while/body/eval_jaxpr/rhd,khd->hrk/dot_general | solution.py:66
  125.2 2.1 fusion.50
  128.4 8.7 %fusion.51 = bf16[640,5,128]{0,2,1:T(8,128)(2,1)S(1)} fusion(f32[5,640]{1,0:T(8,128)S(1)} %fusion.50, bf16[640,15,128]{2,0,1:T(8,128)(2,1)} %get-tuple-element.230, s32[]{:T(128)S(6)} %select_n.242, f32[5,640,640]{1,2,0:T(8,128)} %copy-done.3), kind=kOutput, calls=%fused_computation.17.clone.1 | convolution fusion | flops 534941440 | bytes 18035204 | tf_op jit(solution)/shard_map/while/body/eval_jaxpr/hrk,khd->rhd/dot_general | solution.py:70
  137.0 1.4 copy.207
  139.4 2.6 %fusion.49 = f32[5,640,640]{1,2,0:T(8,128)S(1)} fusion(bf16[640,15,128]{2,0,1:T(8,128)(2,1)} %get-tuple-element.232, s32[]{:T(128)S(6)} %select_n.242, bf16[640,15,128]{2,0,1:T(8,128)(2,1)} %get-tuple-element.231), kind=kOutput, calls=%fused_computation.18.clone.1 | convolution fusion | flops 524288000 | bytes 9831424 | tf_op jit(solution)/shard_map/while/body/eval_jaxpr/rhd,khd->hrk/dot_general | solution.py:66
  142.0 2.1 fusion.50
  145.2 8.7 %fusion.51 = bf16[640,5,128]{0,2,1:T(8,128)(2,1)S(1)} fusion(f32[5,640]{1,0:T(8,128)S(1)} %fusion.50, bf16[640,15,128]{2,0,1:T(8,128)(2,1)} %get-tuple-element.230, s32[]{:T(128)S(6)} %select_n.242, f32[5,640,640]{1,2,0:T(8,128)} %copy-done.3), kind=kOutput, calls=%fused_computation.17.clone.1 | convolution fusion | flops 534941440 | bytes 18035204 | tf_op jit(solution)/shard_map/while/body/eval_jaxpr/hrk,khd->rhd/dot_general | solution.py:70
  153.8 1.4 copy.207
  156.2 3.3 %constant_dynamic-slice_fusion.17 = (bf16[320,15,128]{2,0,1:T(8,128)(2,1)}, bf16[320,15,128]{2,0,1:T(8,128)(2,1)}) fusion(bf16[640,15,128]{2,0,1:T(8,128)(2,1)} %get-tuple-element.105, s32[]{:T(128)S(6)} %select_n.162, s32[]{:T(128)S(6)} %select_n.163), kind=kLoop, calls=%fused_computation.103 | loop fusion | bytes 4915208 | tf_op jit(solution)/shard_map/dynamic_slice | solution.py:165
  159.8 4.6 %exponential_reduce_fusion = (f32[2,20,10,8]{3,2,1,0:T(8,128)S(1)}, f32[2,20,10,8,8]{3,4,2,1,0:T(8,128)}) fusion(bf16[8,2,20,10,128]{4,3,2,1,0:T(8,128)(2,1)} %bitcast.13, bf16[8,2,20,10,128]{4,3,2,1,0:T(8,128)(2,1)} %bitcast.10, pred[10,8,8]{1,2,0:T(8,128)(4,1)S(1)} %broadcast_compare_fusion), kind=kOutput, calls=%fused_computation.44 | convolution fusion | flops 6656007 | bytes 1754240 | tf_op jit(solution)/shard_map/sub | solution.py:44
  164.5 2.3 %fusion.24 = bf16[8,2,20,10,128]{4,0,3,2,1:T(8,128)(2,1)S(1)} fusion(bf16[8,2,20,10,128]{4,3,2,1,0:T(8,128)(2,1)S(1)} %bitcast.133, f32[2,20,10,8,8]{3,4,2,1,0:T(8,128)} %get-tuple-element.176, f32[2,20,10,8]{3,2,1,0:T(8,128)S(1)} %get-tuple-element.175), kind=kOutput, calls=%fused_computation.46 | convolution fusion | flops 7014400 | bytes 1753600 | tf_op jit(solution)/shard_map/apnfg,gapnd->fapnd/dot_general | solution.py:103
  166.8 1.3 copy.126
  168.1 1.9 constant_dynamic-slice_fusion
  170.3 1.3 collective-permute-start.5
  172.8 1.6 collective-permute-start.8
  174.3 1.2 collective-permute-start.9
  176.2 1.4 collective-permute-start.10
  177.6 2.1 collective-permute-start.11
  180.0 3.1 %collective-permute-start.13 = (bf16[1,20,10,128]{3,1,2,0:T(8,128)(2,1)S(1)}, bf16[1,20,10,128]{3,1,2,0:T(8,128)(2,1)S(1)}, u32[]{:S(2)}, u32[]{:S(2)}) collective-permute-start(bf16[1,20,10,128]{3,1,2,0:T(8,128)(2,1)S(1)} %bitcast.139), channel_id=1, source_target_pairs={{0,10},{1,11},{2,8},{3,9},{4,14},{5,15},{6,12},{7,13},{8,2},{9,3},... | collective-permute-start | bytes 153608 | tf_op jit(solution)/shard_map/ppermute | solution.py:115
  184.2 1.3 collective-permute-start.15
  185.5 2.5 %collective-permute-done.12 = bf16[1,20,10,128]{3,1,2,0:T(8,128)(2,1)S(1)} collective-permute-done((bf16[1,20,10,128]{3,1,2,0:T(8,128)(2,1)S(1)}, bf16[1,20,10,128]{3,1,2,0:T(8,128)(2,1)S(1)}, u32[]{:S(2)}, u32[]{:S(2)}) %collective-permute-start.12) | collective-permute-done | bytes 51232 | tf_op jit(solution)/shard_map/ppermute | solution.py:115
  188.0 1.8 collective-permute-done.13
  191.8 1.5 collective-permute-start.18
  193.3 1.1 collective-permute-done.15
  194.4 2.5 %collective-permute-done.16 = bf16[1,20,10,128]{3,1,2,0:T(8,128)(2,1)S(1)} collective-permute-done((bf16[1,20,10,128]{3,1,2,0:T(8,128)(2,1)S(1)}, bf16[1,20,10,128]{3,1,2,0:T(8,128)(2,1)S(1)}, u32[]{:S(2)}, u32[]{:S(2)}) %collective-permute-start.16) | collective-permute-done | bytes 51232 | tf_op jit(solution)/shard_map/ppermute | solution.py:115
  196.9 3.2 %collective-permute-done.17 = bf16[1,20,10,128]{3,1,2,0:T(8,128)(2,1)S(1)} collective-permute-done((bf16[1,20,10,128]{3,1,2,0:T(8,128)(2,1)S(1)}, bf16[1,20,10,128]{3,1,2,0:T(8,128)(2,1)S(1)}, u32[]{:S(2)}, u32[]{:S(2)}) %collective-permute-start.17) | collective-permute-done | bytes 51232 | tf_op jit(solution)/shard_map/ppermute | solution.py:115
  200.2 2.6 %collective-permute-done.18 = bf16[1,20,10,128]{3,1,2,0:T(8,128)(2,1)S(1)} collective-permute-done((bf16[1,20,10,128]{3,1,2,0:T(8,128)(2,1)S(1)}, bf16[1,20,10,128]{3,1,2,0:T(8,128)(2,1)S(1)}, u32[]{:S(2)}, u32[]{:S(2)}) %collective-permute-start.18) | collective-permute-done | bytes 51232 | tf_op jit(solution)/shard_map/ppermute | solution.py:115
  203.9 2.6 %maximum_select_fusion.3 = bf16[320,30,128]{2,0,1:T(8,128)(2,1)S(1)} fusion(bf16[320,15,128]{2,0,1:T(8,128)(2,1)} %collective-permute-done.3, bf16[320,15,128]{2,0,1:T(8,128)(2,1)} %get-tuple-element.145, pred[]{:T(512)S(6)} %eq.4), kind=kLoop, calls=%fused_computation.37 | loop fusion | flops 3686400 | bytes 4915201 | tf_op jit(solution)/shard_map/jit(_where)/select_n | solution.py:168
  206.6 2.0 pad_maximum_fusion
  208.6 4.9 %gather_fusion.2 = bf16[40,320,128]{2,1,0:T(8,128)(2,1)} fusion(bf16[320,40,128]{2,0,1:T(8,128)(2,1)} %pad_maximum_fusion, s32[1024]{0:T(1024)S(1)} %pad_clamp_fusion), kind=kCustom, calls=%fused_computation.8 | custom fusion | bytes 6553760 | tf_op jit(solution)/shard_map/jit(_take)/gather | solution.py:173
  213.5 4.3 %bitcast_select_fusion = bf16[320,5120]{1,0:T(8,128)(2,1)} fusion(pred[5120]{0:T(1024)(128)(4,1)S(1)} %broadcast_bitcast_fusion, bf16[40,320,128]{2,1,0:T(8,128)(2,1)} %gather_fusion.2), kind=kLoop, calls=%fused_computation.29 | loop fusion | flops 1638400 | bytes 6558720 | tf_op jit(solution)/shard_map/jit(_take)/select_n | solution.py:173
  (109 shorter events, 15.4 us)
Async XLA Ops:
  0.0 2.9 %copy-start = (bf16[320,5120]{1,0:T(8,128)(2,1)S(1)}, bf16[320,5120]{1,0:T(8,128)(2,1)}, u32[]{:S(2)}) copy-start(bf16[320,5120]{1,0:T(8,128)(2,1)} %param.11) | copy-start | bytes 9830404
  2.9 2.6 %copy-start.13 = (bf16[320,5120]{1,0:T(8,128)(2,1)S(1)}, bf16[320,5120]{1,0:T(8,128)(2,1)}, u32[]{:S(2)}) copy-start(bf16[320,5120]{1,0:T(8,128)(2,1)} %param.12) | copy-start | bytes 9830404
  5.6 2.6 %copy-start.4 = (bf16[320,40,128]{2,0,1:T(8,128)(2,1)S(1)}, bf16[320,40,128]{2,0,1:T(8,128)(2,1)}, u32[]{:S(2)}) copy-start(bf16[320,40,128]{2,0,1:T(8,128)(2,1)} %copy_bitcast_fusion.1) | copy-start | bytes 9830404
  26.2 36.9 %all-to-all-start.2 = ((bf16[1,320,10,128]{3,2,0,1:T(8,128)(2,1)}), bf16[1,320,10,128]{3,2,0,1:T(8,128)(2,1)}, u32[]{:S(2)}, u32[]{:S(2)}) async-start(bf16[1,320,10,128]{3,2,0,1:T(8,128)(2,1)} %copy.120), calls=%async_computation.2 | async-start | bytes 2621440 | tf_op jit(solution)/shard_map/all_to_all | solution.py:82
  39.4 4.4 %copy-start.5 = (bf16[30,320,128]{2,1,0:T(8,128)(2,1)S(1)}, bf16[30,320,128]{2,1,0:T(8,128)(2,1)}, u32[]{:S(2)}) copy-start(bf16[30,320,128]{2,1,0:T(8,128)(2,1)} %gather_fusion.5) | copy-start | bytes 7372804
  49.6 3.8 %copy-start.7 = (bf16[320,30,128]{2,0,1:T(8,128)(2,1)S(1)}, bf16[320,30,128]{2,0,1:T(8,128)(2,1)}, u32[]{:S(2)}) copy-start(bf16[320,30,128]{2,0,1:T(8,128)(2,1)} %get-tuple-element.170) | copy-start | bytes 7372804
  53.1 17.9 %collective-permute-start = (bf16[320,15,128]{2,0,1:T(8,128)(2,1)}, bf16[320,15,128]{2,0,1:T(8,128)(2,1)}, u32[]{:S(2)}, u32[]{:S(2)}) collective-permute-start(bf16[320,15,128]{2,0,1:T(8,128)(2,1)} %get-tuple-element.152), channel_id=1, source_target_pairs={{0,1},{1,0},{2,3},{3,2},{4,5},{5,4},{6,7},{7,6},{8,9},{9,8},{10,11... | collective-permute-start | bytes 3686408 | tf_op jit(solution)/shard_map/ppermute | solution.py:39
  53.4 2.6 %copy-start.6 = (bf16[320,30,128]{2,0,1:T(8,128)(2,1)S(1)}, bf16[320,30,128]{2,0,1:T(8,128)(2,1)}, u32[]{:S(2)}) copy-start(bf16[320,30,128]{2,0,1:T(8,128)(2,1)} %get-tuple-element.169) | copy-start | bytes 7372804
  55.0 20.0 %collective-permute-start.1 = (bf16[320,15,128]{2,0,1:T(8,128)(2,1)}, bf16[320,15,128]{2,0,1:T(8,128)(2,1)}, u32[]{:S(2)}, u32[]{:S(2)}) collective-permute-start(bf16[320,15,128]{2,0,1:T(8,128)(2,1)} %get-tuple-element.150), channel_id=1, source_target_pairs={{0,1},{1,0},{2,3},{3,2},{4,5},{5,4},{6,7},{7,6},{8,9},{9,8},{10,11... | collective-permute-start | bytes 3686408 | tf_op jit(solution)/shard_map/ppermute | solution.py:39
  56.0 3.8 %copy-start.12 = (bf16[1,320,10,128]{3,1,2,0:T(8,128)(2,1)S(1)}, bf16[1,320,10,128]{3,1,2,0:T(8,128)(2,1)}, u32[]{:S(2)}) copy-start(bf16[1,320,10,128]{3,1,2,0:T(8,128)(2,1)} %get-tuple-element.172) | copy-start | bytes 2457604
  57.6 10.8 %copy-start.11 = (bf16[1,320,10,128]{3,1,2,0:T(8,128)(2,1)S(1)}, bf16[1,320,10,128]{3,1,2,0:T(8,128)(2,1)}, u32[]{:S(2)}) copy-start(bf16[1,320,10,128]{3,1,2,0:T(8,128)(2,1)} %get-tuple-element.174) | copy-start | bytes 2457604
  57.6 21.4 %collective-permute-start.2 = (bf16[320,15,128]{2,0,1:T(8,128)(2,1)}, bf16[320,15,128]{2,0,1:T(8,128)(2,1)}, u32[]{:S(2)}, u32[]{:S(2)}) collective-permute-start(bf16[320,15,128]{2,0,1:T(8,128)(2,1)} %get-tuple-element.148), channel_id=1, source_target_pairs={{0,1},{1,0},{2,3},{3,2},{4,5},{5,4},{6,7},{7,6},{8,9},{9,8},{10,11... | collective-permute-start | bytes 3686408 | tf_op jit(solution)/shard_map/ppermute | solution.py:39
  61.4 8.6 %copy-start.2 = (s32[40]{0:T(128)S(1)}, s32[40]{0:T(128)}, u32[]{:S(2)}) copy-start(s32[40]{0:T(128)} %param.15) | copy-start | bytes 484
  61.5 9.5 %copy-start.8 = (bf16[320,15,128]{2,0,1:T(8,128)(2,1)S(1)}, bf16[320,15,128]{2,0,1:T(8,128)(2,1)}, u32[]{:S(2)}) copy-start(bf16[320,15,128]{2,0,1:T(8,128)(2,1)} %get-tuple-element.151) | copy-start | bytes 3686404
  63.1 35.5 %all-to-all-start.1 = ((bf16[1,320,10,128]{3,2,0,1:T(8,128)(2,1)}), bf16[1,320,10,128]{3,2,0,1:T(8,128)(2,1)}, u32[]{:S(2)}, u32[]{:S(2)}) async-start(bf16[1,320,10,128]{3,2,0,1:T(8,128)(2,1)} %copy.117), calls=%async_computation.1 | async-start | bytes 2621440 | tf_op jit(solution)/shard_map/all_to_all | solution.py:81
  71.0 4.0 %copy-start.9 = (bf16[320,15,128]{2,0,1:T(8,128)(2,1)S(1)}, bf16[320,15,128]{2,0,1:T(8,128)(2,1)}, u32[]{:S(2)}) copy-start(bf16[320,15,128]{2,0,1:T(8,128)(2,1)} %get-tuple-element.149) | copy-start | bytes 3686404
  75.0 4.0 %copy-start.10 = (bf16[320,15,128]{2,0,1:T(8,128)(2,1)S(1)}, bf16[320,15,128]{2,0,1:T(8,128)(2,1)}, u32[]{:S(2)}) copy-start(bf16[320,15,128]{2,0,1:T(8,128)(2,1)} %get-tuple-element.147) | copy-start | bytes 3686404
  98.6 65.9 %all-to-all-start = ((bf16[1,320,10,128]{3,2,0,1:T(8,128)(2,1)}), bf16[1,320,10,128]{3,2,0,1:T(8,128)(2,1)S(1)}, u32[]{:S(2)}, u32[]{:S(2)}) async-start(bf16[1,320,10,128]{3,2,0,1:T(8,128)(2,1)} %copy.114), calls=%async_computation | async-start | bytes 2621440 | tf_op jit(solution)/shard_map/all_to_all | solution.py:83
  108.4 3.2 %copy-start.3 = (f32[5,640,640]{1,2,0:T(8,128)}, f32[5,640,640]{1,2,0:T(8,128)S(1)}, u32[]{:S(2)}) copy-start(f32[5,640,640]{1,2,0:T(8,128)S(1)} %fusion.49) | copy-start | bytes 24576004 | tf_op jit(solution)/shard_map/while
  125.2 3.2 %copy-start.3 = (f32[5,640,640]{1,2,0:T(8,128)}, f32[5,640,640]{1,2,0:T(8,128)S(1)}, u32[]{:S(2)}) copy-start(f32[5,640,640]{1,2,0:T(8,128)S(1)} %fusion.49) | copy-start | bytes 24576004 | tf_op jit(solution)/shard_map/while
  142.0 3.2 %copy-start.3 = (f32[5,640,640]{1,2,0:T(8,128)}, f32[5,640,640]{1,2,0:T(8,128)S(1)}, u32[]{:S(2)}) copy-start(f32[5,640,640]{1,2,0:T(8,128)S(1)} %fusion.49) | copy-start | bytes 24576004 | tf_op jit(solution)/shard_map/while
  159.5 44.5 %collective-permute-start.3 = (bf16[320,15,128]{2,0,1:T(8,128)(2,1)}, bf16[320,15,128]{2,0,1:T(8,128)(2,1)}, u32[]{:S(2)}, u32[]{:S(2)}) collective-permute-start(bf16[320,15,128]{2,0,1:T(8,128)(2,1)} %get-tuple-element.146), channel_id=1, source_target_pairs={{0,1},{1,0},{2,3},{3,2},{4,5},{5,4},{6,7},{7,6},{8,9},{9,8},{10,11... | collective-permute-start | bytes 3686408 | tf_op jit(solution)/shard_map/ppermute | solution.py:39
  170.0 2.7 %collective-permute-start.4 = (bf16[1,20,10,128]{3,1,2,0:T(8,128)(2,1)S(1)}, bf16[1,20,10,128]{3,1,2,0:T(8,128)(2,1)S(1)}, u32[]{:S(2)}, u32[]{:S(2)}) collective-permute-start(bf16[1,20,10,128]{3,1,2,0:T(8,128)(2,1)S(1)} %bitcast.148), channel_id=1, source_target_pairs={{0,1},{1,0},{2,3},{3,2},{4,5},{5,4},{6,7},{7,6},{8,9},{9,8},{10,11... | collective-permute-start | bytes 153608 | tf_op jit(solution)/shard_map/ppermute | solution.py:115
  170.3 4.1 %collective-permute-start.5 = (bf16[1,20,10,128]{3,1,2,0:T(8,128)(2,1)S(1)}, bf16[1,20,10,128]{3,1,2,0:T(8,128)(2,1)S(1)}, u32[]{:S(2)}, u32[]{:S(2)}) collective-permute-start(bf16[1,20,10,128]{3,1,2,0:T(8,128)(2,1)S(1)} %bitcast.147), channel_id=1, source_target_pairs={{0,2},{1,3},{2,0},{3,1},{4,6},{5,7},{6,4},{7,5},{8,10},{9,11},{10,... | collective-permute-start | bytes 153608 | tf_op jit(solution)/shard_map/ppermute | solution.py:115
  171.5 4.6 %collective-permute-start.6 = (bf16[1,20,10,128]{3,1,2,0:T(8,128)(2,1)S(1)}, bf16[1,20,10,128]{3,1,2,0:T(8,128)(2,1)S(1)}, u32[]{:S(2)}, u32[]{:S(2)}) collective-permute-start(bf16[1,20,10,128]{3,1,2,0:T(8,128)(2,1)S(1)} %bitcast.146), channel_id=1, source_target_pairs={{0,3},{1,2},{2,1},{3,0},{4,7},{5,6},{6,5},{7,4},{8,11},{9,10},{10,... | collective-permute-start | bytes 153608 | tf_op jit(solution)/shard_map/ppermute | solution.py:115
  172.4 5.1 %collective-permute-start.7 = (bf16[1,20,10,128]{3,1,2,0:T(8,128)(2,1)S(1)}, bf16[1,20,10,128]{3,1,2,0:T(8,128)(2,1)S(1)}, u32[]{:S(2)}, u32[]{:S(2)}) collective-permute-start(bf16[1,20,10,128]{3,1,2,0:T(8,128)(2,1)S(1)} %bitcast.145), channel_id=1, source_target_pairs={{0,4},{1,5},{2,6},{3,7},{4,0},{5,1},{6,2},{7,3},{8,12},{9,13},{10,... | collective-permute-start | bytes 153608 | tf_op jit(solution)/shard_map/ppermute | solution.py:115
  172.8 7.0 %collective-permute-start.8 = (bf16[1,20,10,128]{3,1,2,0:T(8,128)(2,1)S(1)}, bf16[1,20,10,128]{3,1,2,0:T(8,128)(2,1)S(1)}, u32[]{:S(2)}, u32[]{:S(2)}) collective-permute-start(bf16[1,20,10,128]{3,1,2,0:T(8,128)(2,1)S(1)} %bitcast.144), channel_id=1, source_target_pairs={{0,5},{1,4},{2,7},{3,6},{4,1},{5,0},{6,3},{7,2},{8,13},{9,12},{10,... | collective-permute-start | bytes 153608 | tf_op jit(solution)/shard_map/ppermute | solution.py:115
  174.3 5.6 %collective-permute-start.9 = (bf16[1,20,10,128]{3,1,2,0:T(8,128)(2,1)S(1)}, bf16[1,20,10,128]{3,1,2,0:T(8,128)(2,1)S(1)}, u32[]{:S(2)}, u32[]{:S(2)}) collective-permute-start(bf16[1,20,10,128]{3,1,2,0:T(8,128)(2,1)S(1)} %bitcast.143), channel_id=1, source_target_pairs={{0,6},{1,7},{2,4},{3,5},{4,2},{5,3},{6,0},{7,1},{8,14},{9,15},{10,... | collective-permute-start | bytes 153608 | tf_op jit(solution)/shard_map/ppermute | solution.py:115
  176.2 6.9 %collective-permute-start.10 = (bf16[1,20,10,128]{3,1,2,0:T(8,128)(2,1)S(1)}, bf16[1,20,10,128]{3,1,2,0:T(8,128)(2,1)S(1)}, u32[]{:S(2)}, u32[]{:S(2)}) collective-permute-start(bf16[1,20,10,128]{3,1,2,0:T(8,128)(2,1)S(1)} %bitcast.142), channel_id=1, source_target_pairs={{0,7},{1,6},{2,5},{3,4},{4,3},{5,2},{6,1},{7,0},{8,15},{9,14},{10,... | collective-permute-start | bytes 153608 | tf_op jit(solution)/shard_map/ppermute | solution.py:115
  177.6 6.6 %collective-permute-start.11 = (bf16[1,20,10,128]{3,1,2,0:T(8,128)(2,1)S(1)}, bf16[1,20,10,128]{3,1,2,0:T(8,128)(2,1)S(1)}, u32[]{:S(2)}, u32[]{:S(2)}) collective-permute-start(bf16[1,20,10,128]{3,1,2,0:T(8,128)(2,1)S(1)} %bitcast.141), channel_id=1, source_target_pairs={{0,8},{1,9},{2,10},{3,11},{4,12},{5,13},{6,14},{7,15},{8,0},{9,1},... | collective-permute-start | bytes 153608 | tf_op jit(solution)/shard_map/ppermute | solution.py:115
  179.7 8.2 %collective-permute-start.12 = (bf16[1,20,10,128]{3,1,2,0:T(8,128)(2,1)S(1)}, bf16[1,20,10,128]{3,1,2,0:T(8,128)(2,1)S(1)}, u32[]{:S(2)}, u32[]{:S(2)}) collective-permute-start(bf16[1,20,10,128]{3,1,2,0:T(8,128)(2,1)S(1)} %bitcast.140), channel_id=1, source_target_pairs={{0,9},{1,8},{2,11},{3,10},{4,13},{5,12},{6,15},{7,14},{8,1},{9,0},... | collective-permute-start | bytes 153608 | tf_op jit(solution)/shard_map/ppermute | solution.py:115
  180.0 9.8 %collective-permute-start.13 = (bf16[1,20,10,128]{3,1,2,0:T(8,128)(2,1)S(1)}, bf16[1,20,10,128]{3,1,2,0:T(8,128)(2,1)S(1)}, u32[]{:S(2)}, u32[]{:S(2)}) collective-permute-start(bf16[1,20,10,128]{3,1,2,0:T(8,128)(2,1)S(1)} %bitcast.139), channel_id=1, source_target_pairs={{0,10},{1,11},{2,8},{3,9},{4,14},{5,15},{6,12},{7,13},{8,2},{9,3},... | collective-permute-start | bytes 153608 | tf_op jit(solution)/shard_map/ppermute | solution.py:115
  183.1 8.7 %collective-permute-start.14 = (bf16[1,20,10,128]{3,1,2,0:T(8,128)(2,1)S(1)}, bf16[1,20,10,128]{3,1,2,0:T(8,128)(2,1)S(1)}, u32[]{:S(2)}, u32[]{:S(2)}) collective-permute-start(bf16[1,20,10,128]{3,1,2,0:T(8,128)(2,1)S(1)} %bitcast.138), channel_id=1, source_target_pairs={{0,11},{1,10},{2,9},{3,8},{4,15},{5,14},{6,13},{7,12},{8,3},{9,2},... | collective-permute-start | bytes 153608 | tf_op jit(solution)/shard_map/ppermute | solution.py:115
  184.2 10.2 %collective-permute-start.15 = (bf16[1,20,10,128]{3,1,2,0:T(8,128)(2,1)S(1)}, bf16[1,20,10,128]{3,1,2,0:T(8,128)(2,1)S(1)}, u32[]{:S(2)}, u32[]{:S(2)}) collective-permute-start(bf16[1,20,10,128]{3,1,2,0:T(8,128)(2,1)S(1)} %bitcast.137), channel_id=1, source_target_pairs={{0,12},{1,13},{2,14},{3,15},{4,8},{5,9},{6,10},{7,11},{8,4},{9,5},... | collective-permute-start | bytes 153608 | tf_op jit(solution)/shard_map/ppermute | solution.py:115
  187.9 9.0 %collective-permute-start.16 = (bf16[1,20,10,128]{3,1,2,0:T(8,128)(2,1)S(1)}, bf16[1,20,10,128]{3,1,2,0:T(8,128)(2,1)S(1)}, u32[]{:S(2)}, u32[]{:S(2)}) collective-permute-start(bf16[1,20,10,128]{3,1,2,0:T(8,128)(2,1)S(1)} %bitcast.136), channel_id=1, source_target_pairs={{0,13},{1,12},{2,15},{3,14},{4,9},{5,8},{6,11},{7,10},{8,5},{9,4},... | collective-permute-start | bytes 153608 | tf_op jit(solution)/shard_map/ppermute | solution.py:115
  189.8 10.4 %collective-permute-start.17 = (bf16[1,20,10,128]{3,1,2,0:T(8,128)(2,1)S(1)}, bf16[1,20,10,128]{3,1,2,0:T(8,128)(2,1)S(1)}, u32[]{:S(2)}, u32[]{:S(2)}) collective-permute-start(bf16[1,20,10,128]{3,1,2,0:T(8,128)(2,1)S(1)} %bitcast.135), channel_id=1, source_target_pairs={{0,14},{1,15},{2,12},{3,13},{4,10},{5,11},{6,8},{7,9},{8,6},{9,7},... | collective-permute-start | bytes 153608 | tf_op jit(solution)/shard_map/ppermute | solution.py:115
  191.8 11.0 %collective-permute-start.18 = (bf16[1,20,10,128]{3,1,2,0:T(8,128)(2,1)S(1)}, bf16[1,20,10,128]{3,1,2,0:T(8,128)(2,1)S(1)}, u32[]{:S(2)}, u32[]{:S(2)}) collective-permute-start(bf16[1,20,10,128]{3,1,2,0:T(8,128)(2,1)S(1)} %bitcast.134), channel_id=1, source_target_pairs={{0,15},{1,14},{2,13},{3,12},{4,11},{5,10},{6,9},{7,8},{8,7},{9,6},... | collective-permute-start | bytes 153608 | tf_op jit(solution)/shard_map/ppermute | solution.py:115
  208.6 9.2 %copy-start.1 = (bf16[320,5120]{1,0:T(8,128)(2,1)S(1)}, bf16[320,5120]{1,0:T(8,128)(2,1)}, u32[]{:S(2)}) copy-start(bf16[320,5120]{1,0:T(8,128)(2,1)} %param.11) | copy-start | bytes 9830404
